TPU v7x, 128 devices: a whole 4x4x4 slice. The times are simulated.
128 devices in a mesh: dp: 4 (over y), seq: 32 (over x, z, core).
Axes of the slice: x: 4, y: 4, z: 4, core: 2. Of those that a mesh axis runs over, the one named last changes fastest.
Arguments:
- tokens: bfloat16 [4, 16384, 1024], P('dp', 'seq'), may hold values from -18 to 18
- lengths: int32 [4, 128], P('dp'), may hold values from 1 to 128
- w_query: bfloat16 [1024, 512], replicated, may hold values from -0.1875 to 0.1875
- w_key: bfloat16 [1024, 512], replicated, may hold values from -0.1875 to 0.1875
- w_value: bfloat16 [1024, 512], replicated, may hold values from -0.1875 to 0.1875
- w_out: bfloat16 [512, 1024], replicated, may hold values from -2 to 2
- cotangent: bfloat16 [4, 16384, 1024], P('dp', 'seq'), may hold values from -6 to 6
Outputs:
- mixed: bfloat16 [4, 16384, 1024], P('dp', 'seq')
- grad_tokens: bfloat16 [4, 16384, 1024], P('dp', 'seq')
- grad_query: float32 [1024, 512], replicated
- grad_key: float32 [1024, 512], replicated
- grad_value: float32 [1024, 512], replicated
- grad_output: float32 [512, 1024], replicated
All inputs are finite; a program needn't handle non-finite values.
Results may differ from a plain program's by a relative error of at most 0.014.
The roundings to bfloat16 on the way count: a program that leaves them out, or rounds other values in their place, can miss the bound.
Values may be sent and summed in bfloat16 or wider, within the bound.
A program may use at most 192 MiB of HBM per device.

v0:
```python
import math
import jax
import jax.numpy as jnp
from jax import lax
from jax.sharding import PartitionSpec as P

HEADS = 4
TILE = 128
bar_offsets = (0, 1, 2, 4, 8, 12, 16, 24, 32)
group_bars = 4
far_score = -1e30


def sent_to_all(shard, axis):
    count = lax.axis_size(axis)
    return lax.all_to_all(
        jnp.broadcast_to(shard[None], (count, *shard.shape)), axis, 0, 0, tiled=True
    )


def joined_along(parts, dim):
    parts = jnp.moveaxis(parts, 0, dim)
    shape = parts.shape
    return parts.reshape(*shape[:dim], shape[dim] * shape[dim + 1], *shape[dim + 2 :])


def collect(shard, axis, dim):
    parts = sent_to_all(shard, axis)
    return joined_along(parts, dim)


def side_by_side(arrays, axis, dim, along):
    both = jnp.concatenate(arrays, axis=along)
    whole, at, gathered = (collect(both, axis, dim), 0, [])
    for a in arrays:
        gathered.append(lax.slice_in_dim(whole, at, at + a.shape[along], axis=along))
        at += a.shape[along]
    return tuple(gathered)


def shifted(block, axis, distance):
    devices = range(lax.axis_size(axis))
    route = [(i - distance, i) for i in devices if i - distance in devices]
    return lax.ppermute(block, axis, route)


def split_up(shard, dim, count):
    shape = shard.shape
    parts = shard.reshape(*shape[:dim], count, shape[dim] // count, *shape[dim + 1 :])
    return jnp.moveaxis(parts, dim, 0)


def sent_and_summed(shard, axis, dim):
    parts = split_up(shard, dim, lax.axis_size(axis))
    arrived = lax.all_to_all(parts, axis, split_axis=0, concat_axis=0, tiled=True)
    return arrived.astype(jnp.float32).sum(axis=0)


def in_one_piece(arrays, axis, dim, along):
    ends, at = ([], 0)
    for a in arrays[:-1]:
        at += a.shape[along]
        ends.append(at)
    both = jnp.concatenate(arrays, axis=along)
    return tuple(jnp.split(sent_and_summed(both, axis, dim), ends, axis=along))


def product(form, left, right):
    return jnp.einsum(form, left, right, preferred_element_type=jnp.float32)


def summarize(bar_rows, length):
    slot_ids = jnp.arange(bar_rows.shape[1], dtype=jnp.int32)
    live_slots = slot_ids[None, :] < length[:, None]
    running = jnp.sum(jnp.where(live_slots[:, :, None], bar_rows.astype(jnp.float32), 0.0), axis=1)
    return (running / length[:, None].astype(jnp.float32)).astype(jnp.bfloat16)


def bar_block(
    queries,
    ext_key,
    ext_value,
    ext_length,
    base_bar,
    bar_ids,
    query_length,
    summary_key,
    summary_value,
    grad_context,
):
    group_count, tile_len, head_count, head_dim = queries.shape
    sources = len(bar_offsets)
    key_parts = []
    value_parts = []
    length_parts = []
    for offset in bar_offsets:
        first_bar = base_bar - offset
        key_parts.append(lax.dynamic_slice_in_dim(ext_key, first_bar, group_count, 0))
        value_parts.append(lax.dynamic_slice_in_dim(ext_value, first_bar, group_count, 0))
        length_parts.append(lax.dynamic_slice_in_dim(ext_length, first_bar, group_count, 0))
    fine_key = jnp.stack(key_parts, 1).reshape(
        group_count, sources * tile_len, head_count, head_dim
    )
    fine_value = jnp.stack(value_parts, 1).reshape(
        group_count, sources * tile_len, head_count, head_dim
    )
    fine_length = jnp.stack(length_parts, 1)
    slot_ids = jnp.arange(tile_len, dtype=jnp.int32)
    key_live = slot_ids[None, None, :] < fine_length[:, :, None]
    causal = slot_ids[None, :] <= slot_ids[:, None]
    other_bar = jnp.arange(sources, dtype=jnp.int32) != 0
    fine_live = key_live[:, None, :, :] & (
        causal[None, :, None, :] | other_bar[None, None, :, None]
    )
    fine_live = fine_live.reshape(group_count, 1, tile_len, sources * tile_len)
    distance = bar_ids[:, None] - jnp.arange(summary_key.shape[0], dtype=jnp.int32)[None, :]
    coarse_live = distance >= 1
    for offset in bar_offsets[1:]:
        coarse_live = coarse_live & (distance != offset)
    coarse_live = coarse_live[:, None, None, :]
    score_scale = 1.0 / math.sqrt(head_dim)
    fine_score = product("gqhe,gkhe->ghqk", queries, fine_key) * score_scale
    coarse_score = product("gqhe,nhe->ghqn", queries, summary_key) * score_scale
    fine_score = jnp.where(fine_live, fine_score, far_score)
    coarse_score = jnp.where(coarse_live, coarse_score, far_score)
    top_score = jnp.maximum(jnp.max(fine_score, axis=-1), jnp.max(coarse_score, axis=-1))[..., None]
    fine_exp = jnp.where(fine_live, jnp.exp(fine_score - top_score), 0.0)
    coarse_exp = jnp.where(coarse_live, jnp.exp(coarse_score - top_score), 0.0)
    denominator = (jnp.sum(fine_exp, axis=-1) + jnp.sum(coarse_exp, axis=-1))[..., None]
    fine_prob = fine_exp / denominator
    coarse_prob = coarse_exp / denominator
    fine_round = fine_prob.astype(jnp.bfloat16)
    coarse_round = coarse_prob.astype(jnp.bfloat16)
    attended_context = product("ghqk,gkhe->gqhe", fine_round, fine_value) + product(
        "ghqn,nhe->gqhe", coarse_round, summary_value
    )
    query_live = slot_ids[None, :] < query_length[:, None]
    attended_context = jnp.where(query_live[:, :, None, None], attended_context, 0.0)
    fine_dp = product("gqhe,gkhe->ghqk", grad_context, fine_value)
    coarse_dp = product("gqhe,nhe->ghqn", grad_context, summary_value)
    delta = (jnp.sum(fine_prob * fine_dp, axis=-1) + jnp.sum(coarse_prob * coarse_dp, axis=-1))[
        ..., None
    ]
    fine_ds = (fine_prob * (fine_dp - delta) * score_scale).astype(jnp.bfloat16)
    coarse_ds = (coarse_prob * (coarse_dp - delta) * score_scale).astype(jnp.bfloat16)
    query_gradient_rows = product("ghqk,gkhe->gqhe", fine_ds, fine_key) + product(
        "ghqn,nhe->gqhe", coarse_ds, summary_key
    )
    fine_gk = product("ghqk,gqhe->gkhe", fine_ds, queries).reshape(
        group_count, sources, tile_len, head_count, head_dim
    )
    fine_gv = product("ghqk,gqhe->gkhe", fine_round, grad_context).reshape(
        group_count, sources, tile_len, head_count, head_dim
    )
    coarse_key_gradient = product("ghqn,gqhe->nhe", coarse_ds, queries)
    coarse_value_gradient = product("ghqn,gqhe->nhe", coarse_round, grad_context)
    return (
        attended_context,
        query_gradient_rows,
        fine_gk,
        fine_gv,
        coarse_key_gradient,
        coarse_value_gradient,
    )


def spread(running, grads, base_bar):
    group_count = grads.shape[0]
    for position, offset in enumerate(bar_offsets):
        first_bar = base_bar - offset
        current = lax.dynamic_slice_in_dim(running, first_bar, group_count, 0)
        running = lax.dynamic_update_slice_in_dim(
            running, current + grads[:, position], first_bar, 0
        )
    return running


def local(tokens, lengths, w_query, w_key, w_value, w_out, cotangent):
    inputs = tokens[0]
    grad_out = cotangent[0]
    token_count = inputs.shape[0]
    inner_width = w_query.shape[1]
    head_dim = inner_width // HEADS
    bar_count = token_count // TILE
    reach_dev = max(bar_offsets[-1] // bar_count, 1)
    queries = jnp.dot(inputs, w_query, preferred_element_type=jnp.float32).astype(jnp.bfloat16)
    keys_own = jnp.dot(inputs, w_key, preferred_element_type=jnp.float32).astype(jnp.bfloat16)
    values_own = jnp.dot(inputs, w_value, preferred_element_type=jnp.float32).astype(jnp.bfloat16)
    all_length = lengths[0]
    first_own = lax.axis_index("seq") * bar_count
    local_length = lax.dynamic_slice_in_dim(all_length, first_own, bar_count, 0)
    slot_ids = jnp.arange(TILE, dtype=jnp.int32)
    live_slots = slot_ids[None, :] < local_length[:, None]
    token_live = live_slots.reshape(-1)
    own_summary = (
        summarize(keys_own.reshape(bar_count, TILE, inner_width), local_length),
        summarize(values_own.reshape(bar_count, TILE, inner_width), local_length),
    )
    summary_key, summary_value = side_by_side((own_summary[0], own_summary[1]), "seq", 0, 1)
    summary_key = summary_key.reshape(-1, HEADS, head_dim)
    summary_value = summary_value.reshape(-1, HEADS, head_dim)
    grad_context = jnp.dot(grad_out, w_out.T, preferred_element_type=jnp.float32)
    grad_context = jnp.where(token_live[:, None], grad_context, 0.0).astype(jnp.bfloat16)
    key_list = [keys_own]
    value_list = [values_own]
    for distance in range(1, reach_dev + 1):
        arrived = shifted((keys_own, values_own), "seq", distance)
        key_list.append(arrived[0])
        value_list.append(arrived[1])
    key_stack = jnp.stack(key_list, 0)
    value_stack = jnp.stack(value_list, 0)
    ext_bars = (reach_dev + 1) * bar_count
    ext_key = key_stack[::-1].reshape(ext_bars, TILE, HEADS, head_dim)
    ext_value = value_stack[::-1].reshape(ext_bars, TILE, HEADS, head_dim)
    padded_length = jnp.concatenate([jnp.zeros((reach_dev * bar_count,), jnp.int32), all_length], 0)
    ext_length = lax.dynamic_slice_in_dim(padded_length, first_own, ext_bars, 0)
    query_bars = queries.reshape(bar_count, TILE, HEADS, head_dim)
    grad_bars = grad_context.reshape(bar_count, TILE, HEADS, head_dim)

    def step(carried_state, block_index):
        accumulated_key, accumulated_value, accumulated_summary_key, accumulated_summary_value = (
            carried_state
        )
        begin_bar = block_index * group_bars
        base_bar = reach_dev * bar_count + begin_bar
        bar_ids = first_own + begin_bar + jnp.arange(group_bars, dtype=jnp.int32)
        result = bar_block(
            query_bars,
            ext_key,
            ext_value,
            ext_length,
            base_bar,
            bar_ids,
            local_length,
            summary_key,
            summary_value,
            grad_bars,
        )
        (
            attended_context,
            query_gradient_rows,
            fine_gk,
            fine_gv,
            coarse_key_gradient,
            coarse_value_gradient,
        ) = result
        accumulated_key = spread(accumulated_key, fine_gk, base_bar)
        accumulated_value = spread(accumulated_value, fine_gv, base_bar)
        return (
            (
                accumulated_key,
                accumulated_value,
                accumulated_summary_key + coarse_key_gradient,
                accumulated_summary_value + coarse_value_gradient,
            ),
            (attended_context.astype(jnp.bfloat16), query_gradient_rows.astype(jnp.bfloat16)),
        )

    ext_zero = jnp.zeros((ext_bars, TILE, HEADS, head_dim), jnp.float32)
    sum_zero = jnp.zeros(summary_key.shape, jnp.float32)
    carried_state, stacked = lax.scan(
        step,
        (ext_zero, ext_zero, sum_zero, sum_zero),
        jnp.arange(bar_count // group_bars, dtype=jnp.int32),
    )
    accumulated_key, accumulated_value, accumulated_summary_key, accumulated_summary_value = (
        carried_state
    )
    attended_context = stacked[0].reshape(token_count, inner_width)
    query_gradient_rows = stacked[1].reshape(token_count, inner_width)
    grad_key_stack = accumulated_key.reshape(reach_dev + 1, token_count, inner_width)[::-1]
    grad_value_stack = accumulated_value.reshape(reach_dev + 1, token_count, inner_width)[::-1]
    own_key = grad_key_stack[0]
    own_value = grad_value_stack[0]
    for distance in range(1, reach_dev + 1):
        returned = (
            shifted(grad_key_stack[distance].astype(jnp.bfloat16), "seq", -distance).astype(
                jnp.float32
            ),
            shifted(grad_value_stack[distance].astype(jnp.bfloat16), "seq", -distance).astype(
                jnp.float32
            ),
        )
        own_key = own_key + returned[0]
        own_value = own_value + returned[1]
    summary_back = in_one_piece(
        (
            accumulated_summary_key.astype(jnp.bfloat16),
            accumulated_summary_value.astype(jnp.bfloat16),
        ),
        "seq",
        0,
        1,
    )
    inverse_denominator = 1.0 / local_length.astype(jnp.float32)
    shared_key_rows = summary_back[0].reshape(bar_count, inner_width) * inverse_denominator[:, None]
    share_value = summary_back[1].reshape(bar_count, inner_width) * inverse_denominator[:, None]
    own_key = own_key.reshape(bar_count, TILE, inner_width) + jnp.where(
        live_slots[:, :, None], shared_key_rows[:, None, :], 0.0
    )
    own_value = own_value.reshape(bar_count, TILE, inner_width) + jnp.where(
        live_slots[:, :, None], share_value[:, None, :], 0.0
    )
    grad_keys = own_key.reshape(token_count, inner_width).astype(jnp.bfloat16)
    grad_values = own_value.reshape(token_count, inner_width).astype(jnp.bfloat16)
    mixed = jnp.dot(attended_context, w_out, preferred_element_type=jnp.float32).astype(
        jnp.bfloat16
    )
    grad_in = (
        product("te,de->td", query_gradient_rows, w_query)
        + product("te,de->td", grad_keys, w_key)
        + product("te,de->td", grad_values, w_value)
    )
    weight_terms = (
        product("td,te->de", inputs, query_gradient_rows),
        product("td,te->de", inputs, grad_keys),
        product("td,te->de", inputs, grad_values),
        product("te,td->ed", attended_context, grad_out),
    )
    summed = (
        lax.psum(weight_terms[0].astype(jnp.bfloat16), ("dp", "seq")).astype(jnp.float32),
        lax.psum(weight_terms[1].astype(jnp.bfloat16), ("dp", "seq")).astype(jnp.float32),
        lax.psum(weight_terms[2].astype(jnp.bfloat16), ("dp", "seq")).astype(jnp.float32),
        lax.psum(weight_terms[3].astype(jnp.bfloat16), ("dp", "seq")).astype(jnp.float32),
    )
    return (
        mixed[None],
        grad_in.astype(jnp.bfloat16)[None],
        summed[0],
        summed[1],
        summed[2],
        summed[3],
    )


def solution(mesh):
    placed = (P("dp", "seq", None), P("dp", None), P(), P(), P(), P(), P("dp", "seq", None))
    return jax.shard_map(
        local,
        mesh=mesh,
        in_specs=placed,
        out_specs=(P("dp", "seq", None), P("dp", "seq", None), P(), P(), P(), P()),
        check_vma=False,
    )
```

profile of v0, /device:TPU:1, one launch (start us, length us, event | category | flops | bytes accessed | tf_op | source)
XLA Modules:
  0.0 742.3 jit_solution(1753987246523534247)
XLA Ops:
  11.3 4.9 collective-permute-start.15
  16.2 4.0 collective-permute-start.14
  20.2 5.3 collective-permute-start.10
  37.1 4.8 all-to-all-start
  56.2 21.3 %all-to-all-done = bf16[32,4,1024]{2,1,0:T(4,128)(2,1)S(1)} async-done(((bf16[32,4,1024]{2,1,0:T(4,128)(2,1)}), bf16[32,4,1024]{2,1,0:T(4,128)(2,1)S(1)}, u32[]{:S(2)}, u32[]{:S(2)}) %all-to-all-start) | async-done | bytes 262176 | tf_op jit(solution)/shard_map/all_to_all | solution.py:16
  85.3 4.2 collective-permute-start.12
  95.5 4.8 collective-permute-start.7
  101.1 11.5 %collective-permute-done.12 = bf16[512,512]{1,0:T(8,128)(2,1)S(1)} collective-permute-done((bf16[512,512]{1,0:T(8,128)(2,1)}, bf16[512,512]{1,0:T(8,128)(2,1)S(1)}, u32[]{:S(2)}, u32[]{:S(2)}) %collective-permute-start.12) | collective-permute-done | bytes 524320 | tf_op jit(solution)/shard_map/ppermute | solution.py:44
  118.3 6.4 collective-permute-start.4
  125.5 5.2 collective-permute-start.1
  136.4 4.7 rev.9
  141.1 7.7 %reshape.379 = bf16[36,128,4,128]{3,2,1,0:T(4,128)(2,1)} reshape(bf16[9,512,512]{2,1,0:T(8,128)(2,1)} %rev.9) | data formatting | bytes 9437184 | tf_op jit(solution)/shard_map/reshape | solution.py:213
  159.1 25.7 %collective-permute-start.3 = (bf16[512,512]{1,0:T(8,128)(2,1)}, bf16[512,512]{1,0:T(8,128)(2,1)}, u32[]{:S(2)}, u32[]{:S(2)}) collective-permute-start(bf16[512,512]{1,0:T(8,128)(2,1)} %get-tuple-element.136), channel_id=1, source_target_pairs={{0,4},{1,5},{2,6},{3,7},{4,8},{5,9},{6,10},{7,11},{8,12},{9,13},{1... | collective-permute-start | bytes 1572872 | tf_op jit(solution)/shard_map/ppermute | solution.py:44
  216.6 5.7 copy.316
  227.9 4.9 rev.8
  232.7 7.7 %reshape.376 = bf16[36,128,4,128]{3,2,1,0:T(4,128)(2,1)} reshape(bf16[9,512,512]{2,1,0:T(8,128)(2,1)} %rev.8) | data formatting | bytes 9437184 | tf_op jit(solution)/shard_map/reshape | solution.py:214
  242.0 4.6 fusion
  276.0 10.1 %fusion.16 = f32[4,128,4,128]{1,3,2,0:T(8,128)} fusion(bf16[4,1152,4,128]{3,1,2,0:T(8,128)(2,1)} %bitcast.13, f32[4,4,128,1152]{3,2,1,0:T(8,128)} %copy-done.1, f32[4,4,128]{2,1,0:T(4,128)S(1)} %copy_add_fusion.1, f32[4,4,128]{2,1,0:T(4,128)S(1)} %copy_maximum_fusion, pred[4,128,1152]{2,1,0:T(8,128)(4,1)S(1)} %broadcast_and_fusion), kind=kOutput, calls=%fused_computation.36 | convolution fusion | flops 618135552 | bytes 15810560 | tf_op jit(solution)/shard_map/while/body/eval_jaxpr/ghqk,gkhe->gqhe/dot_general | solution.py:69
  286.1 6.9 multiply_reduce_fusion
  293.1 5.9 convolution_bitcast_fusion
  300.4 3.8 multiply_convert_fusion
  306.5 4.9 convolution_bitcast_fusion.1
  311.4 9.6 %copy.338 = f32[4,1152,4,128]{3,1,2,0:T(8,128)} copy(f32[4,1152,4,128]{1,3,2,0:T(8,128)} %convolution_bitcast_fusion.1) | data formatting | bytes 18874368 | tf_op jit(solution)/shard_map/while/body/eval_jaxpr/ghqk,gqhe->gkhe/transpose | solution.py:69
  331.7 3.5 fusion.66
  338.4 10.1 %copy.362 = f32[4,1152,4,128]{3,1,2,0:T(8,128)} copy(f32[4,1152,4,128]{1,3,2,0:T(8,128)} %convolution_bitcast_fusion) | data formatting | bytes 18874368 | tf_op jit(solution)/shard_map/while/body/eval_jaxpr/ghqk,gqhe->gkhe/transpose | solution.py:69
  354.4 14.8 %all-to-all-start.1 = ((bf16[32,4,8,128]{3,1,2,0:T(4,128)(2,1)}), bf16[32,4,8,128]{3,1,2,0:T(4,128)(2,1)S(1)}, u32[]{:S(2)}, u32[]{:S(2)}) async-start(bf16[32,4,8,128]{3,1,2,0:T(4,128)(2,1)} %copy.358), calls=%async_computation.1 | async-start | bytes 524288 | tf_op jit(solution)/shard_map/all_to_all | solution.py:55
  411.4 4.0 convolution_bitcast_fusion.3
  416.7 11.3 %collective-permute-done.22 = bf16[512,512]{1,0:T(8,128)(2,1)} collective-permute-done((bf16[512,512]{1,0:T(8,128)(2,1)}, bf16[512,512]{1,0:T(8,128)(2,1)}, u32[]{:S(2)}, u32[]{:S(2)}) %collective-permute-start.22) | collective-permute-done | bytes 524320 | tf_op jit(solution)/shard_map/ppermute | solution.py:44
  431.3 18.0 %collective-permute-done.23 = bf16[512,512]{1,0:T(8,128)(2,1)} collective-permute-done((bf16[512,512]{1,0:T(8,128)(2,1)}, bf16[512,512]{1,0:T(8,128)(2,1)}, u32[]{:S(2)}, u32[]{:S(2)}) %collective-permute-start.23) | collective-permute-done | bytes 524320 | tf_op jit(solution)/shard_map/ppermute | solution.py:44
  474.5 48.7 %collective-permute-done.30 = bf16[512,512]{1,0:T(8,128)(2,1)} collective-permute-done((bf16[512,512]{1,0:T(8,128)(2,1)}, bf16[512,512]{1,0:T(8,128)(2,1)}, u32[]{:S(2)}, u32[]{:S(2)}) %collective-permute-start.30) | collective-permute-done | bytes 524320 | tf_op jit(solution)/shard_map/ppermute | solution.py:44
  532.8 4.0 collective-permute-done.24
  548.1 178.6 %all-reduce.6.cloned.1.call-done = (bf16[1024,512]{0,1:T(8,128)(2,1)}, bf16[1024,512]{0,1:T(8,128)(2,1)}, bf16[1024,512]{0,1:T(8,128)(2,1)}, bf16[512,1024]{1,0:T(8,128)(2,1)}) async-done(((bf16[1024,512]{0,1:T(8,128)(2,1)}, bf16[1024,512]{0,1:T(8,128)(2,1)}, bf16[1024,512]{0,1:T(8,128)(2,1)}, bf16[512,1024]{1,0:T(8,128)(2,1)}), (bf16[1024,512]{0,1:T(8,128)(2,1)}, bf16[1024,512]{0,1:T(8,128)(2,1)}, ...) | async-done | bytes 4194320 | tf_op jit(solution)/shard_map/psum | solution.py:321
  (330 shorter events, 259.2 us)
Async XLA Ops:
  11.3 121.3 %collective-permute-start.15 = (bf16[512,512]{1,0:T(8,128)(2,1)}, bf16[512,512]{1,0:T(8,128)(2,1)}, u32[]{:S(2)}, u32[]{:S(2)}) collective-permute-start(bf16[512,512]{1,0:T(8,128)(2,1)} %get-tuple-element.138), channel_id=1, source_target_pairs={{0,8},{1,9},{2,10},{3,11},{4,12},{5,13},{6,14},{7,15},{8,16},{9,17... | collective-permute-start | bytes 1572872 | tf_op jit(solution)/shard_map/ppermute | solution.py:44
  16.2 109.3 %collective-permute-start.14 = (bf16[512,512]{1,0:T(8,128)(2,1)}, bf16[512,512]{1,0:T(8,128)(2,1)}, u32[]{:S(2)}, u32[]{:S(2)}) collective-permute-start(bf16[512,512]{1,0:T(8,128)(2,1)} %get-tuple-element.138), channel_id=1, source_target_pairs={{0,7},{1,8},{2,9},{3,10},{4,11},{5,12},{6,13},{7,14},{8,15},{9,16}... | collective-permute-start | bytes 1572872 | tf_op jit(solution)/shard_map/ppermute | solution.py:44
  20.2 71.2 %collective-permute-start.10 = (bf16[512,512]{1,0:T(8,128)(2,1)}, bf16[512,512]{1,0:T(8,128)(2,1)}, u32[]{:S(2)}, u32[]{:S(2)}) collective-permute-start(bf16[512,512]{1,0:T(8,128)(2,1)} %get-tuple-element.138), channel_id=1, source_target_pairs={{0,3},{1,4},{2,5},{3,6},{4,7},{5,8},{6,9},{7,10},{8,11},{9,12},{10... | collective-permute-start | bytes 1572872 | tf_op jit(solution)/shard_map/ppermute | solution.py:44
  25.5 59.8 %collective-permute-start.9 = (bf16[512,512]{1,0:T(8,128)(2,1)}, bf16[512,512]{1,0:T(8,128)(2,1)}, u32[]{:S(2)}, u32[]{:S(2)}) collective-permute-start(bf16[512,512]{1,0:T(8,128)(2,1)} %get-tuple-element.138), channel_id=1, source_target_pairs={{0,2},{1,3},{2,4},{3,5},{4,6},{5,7},{6,8},{7,9},{8,10},{9,11},{10,... | collective-permute-start | bytes 1572872 | tf_op jit(solution)/shard_map/ppermute | solution.py:44
  28.4 52.4 %collective-permute-start.8 = (bf16[512,512]{1,0:T(8,128)(2,1)}, bf16[512,512]{1,0:T(8,128)(2,1)}, u32[]{:S(2)}, u32[]{:S(2)}) collective-permute-start(bf16[512,512]{1,0:T(8,128)(2,1)} %get-tuple-element.138), channel_id=1, source_target_pairs={{0,1},{1,2},{2,3},{3,4},{4,5},{5,6},{6,7},{7,8},{8,9},{9,10},{10,1... | collective-permute-start | bytes 1572872 | tf_op jit(solution)/shard_map/ppermute | solution.py:44
  37.1 40.4 %all-to-all-start = ((bf16[32,4,1024]{2,1,0:T(4,128)(2,1)}), bf16[32,4,1024]{2,1,0:T(4,128)(2,1)S(1)}, u32[]{:S(2)}, u32[]{:S(2)}) async-start(bf16[32,4,1024]{2,1,0:T(4,128)(2,1)} %broadcast_in_dim.191), calls=%async_computation | async-start | bytes 524288 | tf_op jit(solution)/shard_map/all_to_all | solution.py:16
  85.3 27.3 %collective-permute-start.12 = (bf16[512,512]{1,0:T(8,128)(2,1)}, bf16[512,512]{1,0:T(8,128)(2,1)S(1)}, u32[]{:S(2)}, u32[]{:S(2)}) collective-permute-start(bf16[512,512]{1,0:T(8,128)(2,1)} %get-tuple-element.138), channel_id=1, source_target_pairs={{0,5},{1,6},{2,7},{3,8},{4,9},{5,10},{6,11},{7,12},{8,13},{9,14},{... | collective-permute-start | bytes 1572872 | tf_op jit(solution)/shard_map/ppermute | solution.py:44
  91.4 26.9 %collective-permute-start.13 = (bf16[512,512]{1,0:T(8,128)(2,1)}, bf16[512,512]{1,0:T(8,128)(2,1)S(1)}, u32[]{:S(2)}, u32[]{:S(2)}) collective-permute-start(bf16[512,512]{1,0:T(8,128)(2,1)} %get-tuple-element.138), channel_id=1, source_target_pairs={{0,6},{1,7},{2,8},{3,9},{4,10},{5,11},{6,12},{7,13},{8,14},{9,15},... | collective-permute-start | bytes 1572872 | tf_op jit(solution)/shard_map/ppermute | solution.py:44
  95.5 130.5 %collective-permute-start.7 = (bf16[512,512]{1,0:T(8,128)(2,1)}, bf16[512,512]{1,0:T(8,128)(2,1)}, u32[]{:S(2)}, u32[]{:S(2)}) collective-permute-start(bf16[512,512]{1,0:T(8,128)(2,1)} %get-tuple-element.136), channel_id=1, source_target_pairs={{0,8},{1,9},{2,10},{3,11},{4,12},{5,13},{6,14},{7,15},{8,16},{9,17... | collective-permute-start | bytes 1572872 | tf_op jit(solution)/shard_map/ppermute | solution.py:44
  112.6 111.5 %collective-permute-start.6 = (bf16[512,512]{1,0:T(8,128)(2,1)}, bf16[512,512]{1,0:T(8,128)(2,1)}, u32[]{:S(2)}, u32[]{:S(2)}) collective-permute-start(bf16[512,512]{1,0:T(8,128)(2,1)} %get-tuple-element.136), channel_id=1, source_target_pairs={{0,7},{1,8},{2,9},{3,10},{4,11},{5,12},{6,13},{7,14},{8,15},{9,16}... | collective-permute-start | bytes 1572872 | tf_op jit(solution)/shard_map/ppermute | solution.py:44
  118.3 78.3 %collective-permute-start.4 = (bf16[512,512]{1,0:T(8,128)(2,1)}, bf16[512,512]{1,0:T(8,128)(2,1)}, u32[]{:S(2)}, u32[]{:S(2)}) collective-permute-start(bf16[512,512]{1,0:T(8,128)(2,1)} %get-tuple-element.136), channel_id=1, source_target_pairs={{0,5},{1,6},{2,7},{3,8},{4,9},{5,10},{6,11},{7,12},{8,13},{9,14},{... | collective-permute-start | bytes 1572872 | tf_op jit(solution)/shard_map/ppermute | solution.py:44
  125.5 33.5 %collective-permute-start.1 = (bf16[512,512]{1,0:T(8,128)(2,1)}, bf16[512,512]{1,0:T(8,128)(2,1)}, u32[]{:S(2)}, u32[]{:S(2)}) collective-permute-start(bf16[512,512]{1,0:T(8,128)(2,1)} %get-tuple-element.136), channel_id=1, source_target_pairs={{0,2},{1,3},{2,4},{3,5},{4,6},{5,7},{6,8},{7,9},{8,10},{9,11},{10,... | collective-permute-start | bytes 1572872 | tf_op jit(solution)/shard_map/ppermute | solution.py:44
  154.8 35.8 %collective-permute-start.2 = (bf16[512,512]{1,0:T(8,128)(2,1)}, bf16[512,512]{1,0:T(8,128)(2,1)}, u32[]{:S(2)}, u32[]{:S(2)}) collective-permute-start(bf16[512,512]{1,0:T(8,128)(2,1)} %get-tuple-element.136), channel_id=1, source_target_pairs={{0,3},{1,4},{2,5},{3,6},{4,7},{5,8},{6,9},{7,10},{8,11},{9,12},{10... | collective-permute-start | bytes 1572872 | tf_op jit(solution)/shard_map/ppermute | solution.py:44
  159.1 35.7 %collective-permute-start.3 = (bf16[512,512]{1,0:T(8,128)(2,1)}, bf16[512,512]{1,0:T(8,128)(2,1)}, u32[]{:S(2)}, u32[]{:S(2)}) collective-permute-start(bf16[512,512]{1,0:T(8,128)(2,1)} %get-tuple-element.136), channel_id=1, source_target_pairs={{0,4},{1,5},{2,6},{3,7},{4,8},{5,9},{6,10},{7,11},{8,12},{9,13},{1... | collective-permute-start | bytes 1572872 | tf_op jit(solution)/shard_map/ppermute | solution.py:44
  190.6 31.6 %collective-permute-start.5 = (bf16[512,512]{1,0:T(8,128)(2,1)}, bf16[512,512]{1,0:T(8,128)(2,1)}, u32[]{:S(2)}, u32[]{:S(2)}) collective-permute-start(bf16[512,512]{1,0:T(8,128)(2,1)} %get-tuple-element.136), channel_id=1, source_target_pairs={{0,6},{1,7},{2,8},{3,9},{4,10},{5,11},{6,12},{7,13},{8,14},{9,15},... | collective-permute-start | bytes 1572872 | tf_op jit(solution)/shard_map/ppermute | solution.py:44
  354.4 113.5 %all-to-all-start.1 = ((bf16[32,4,8,128]{3,1,2,0:T(4,128)(2,1)}), bf16[32,4,8,128]{3,1,2,0:T(4,128)(2,1)S(1)}, u32[]{:S(2)}, u32[]{:S(2)}) async-start(bf16[32,4,8,128]{3,1,2,0:T(4,128)(2,1)} %copy.358), calls=%async_computation.1 | async-start | bytes 524288 | tf_op jit(solution)/shard_map/all_to_all | solution.py:55
  369.2 357.5 %all-reduce.6.cloned.1.call-start = ((), (), s32[]{:S(2)}) async-start(), calls=%async_computation.2 | async-start | bytes 8388608 | tf_op jit(solution)/shard_map/psum | solution.py:321
  381.9 27.2 %collective-permute-start.17 = (bf16[512,512]{1,0:T(8,128)(2,1)S(1)}, bf16[512,512]{1,0:T(8,128)(2,1)S(1)}, u32[]{:S(2)}, u32[]{:S(2)}) collective-permute-start(bf16[512,512]{1,0:T(8,128)(2,1)S(1)} %bitcast.548), channel_id=1, source_target_pairs={{2,0},{3,1},{4,2},{5,3},{6,4},{7,5},{8,6},{9,7},{10,8},{11,9},{12,... | collective-permute-start | bytes 1572872 | tf_op jit(solution)/shard_map/ppermute | solution.py:44
  383.2 32.3 %collective-permute-start.20 = (bf16[512,512]{1,0:T(8,128)(2,1)}, bf16[512,512]{1,0:T(8,128)(2,1)}, u32[]{:S(2)}, u32[]{:S(2)}) collective-permute-start(bf16[512,512]{1,0:T(8,128)(2,1)} %bitcast.490), channel_id=1, source_target_pairs={{5,0},{6,1},{7,2},{8,3},{9,4},{10,5},{11,6},{12,7},{13,8},{14,9},{... | collective-permute-start | bytes 1572872 | tf_op jit(solution)/shard_map/ppermute | solution.py:44
  384.5 43.6 %collective-permute-start.22 = (bf16[512,512]{1,0:T(8,128)(2,1)}, bf16[512,512]{1,0:T(8,128)(2,1)}, u32[]{:S(2)}, u32[]{:S(2)}) collective-permute-start(bf16[512,512]{1,0:T(8,128)(2,1)} %bitcast.488), channel_id=1, source_target_pairs={{7,0},{8,1},{9,2},{10,3},{11,4},{12,5},{13,6},{14,7},{15,8},{16,9}... | collective-permute-start | bytes 1572872 | tf_op jit(solution)/shard_map/ppermute | solution.py:44
  385.8 44.2 %collective-permute-start.21 = (bf16[512,512]{1,0:T(8,128)(2,1)}, bf16[512,512]{1,0:T(8,128)(2,1)}, u32[]{:S(2)}, u32[]{:S(2)}) collective-permute-start(bf16[512,512]{1,0:T(8,128)(2,1)} %bitcast.489), channel_id=1, source_target_pairs={{6,0},{7,1},{8,2},{9,3},{10,4},{11,5},{12,6},{13,7},{14,8},{15,9},... | collective-permute-start | bytes 1572872 | tf_op jit(solution)/shard_map/ppermute | solution.py:44
  387.1 62.1 %collective-permute-start.23 = (bf16[512,512]{1,0:T(8,128)(2,1)}, bf16[512,512]{1,0:T(8,128)(2,1)}, u32[]{:S(2)}, u32[]{:S(2)}) collective-permute-start(bf16[512,512]{1,0:T(8,128)(2,1)} %bitcast.487), channel_id=1, source_target_pairs={{8,0},{9,1},{10,2},{11,3},{12,4},{13,5},{14,6},{15,7},{16,8},{17,9... | collective-permute-start | bytes 1572872 | tf_op jit(solution)/shard_map/ppermute | solution.py:44
  409.9 40.6 %collective-permute-start.18 = (bf16[512,512]{1,0:T(8,128)(2,1)S(1)}, bf16[512,512]{1,0:T(8,128)(2,1)}, u32[]{:S(2)}, u32[]{:S(2)}) collective-permute-start(bf16[512,512]{1,0:T(8,128)(2,1)S(1)} %bitcast.542), channel_id=1, source_target_pairs={{3,0},{4,1},{5,2},{6,3},{7,4},{8,5},{9,6},{10,7},{11,8},{12,9},{13... | collective-permute-start | bytes 1572872 | tf_op jit(solution)/shard_map/ppermute | solution.py:44
  415.4 52.5 %collective-permute-start.19 = (bf16[512,512]{1,0:T(8,128)(2,1)}, bf16[512,512]{1,0:T(8,128)(2,1)}, u32[]{:S(2)}, u32[]{:S(2)}) collective-permute-start(bf16[512,512]{1,0:T(8,128)(2,1)} %bitcast.491), channel_id=1, source_target_pairs={{4,0},{5,1},{6,2},{7,3},{8,4},{9,5},{10,6},{11,7},{12,8},{13,9},{1... | collective-permute-start | bytes 1572872 | tf_op jit(solution)/shard_map/ppermute | solution.py:44
  428.0 41.2 %collective-permute-start.16 = (bf16[512,512]{1,0:T(8,128)(2,1)}, bf16[512,512]{1,0:T(8,128)(2,1)}, u32[]{:S(2)}, u32[]{:S(2)}) collective-permute-start(bf16[512,512]{1,0:T(8,128)(2,1)} %bitcast.494), channel_id=1, source_target_pairs={{1,0},{2,1},{3,2},{4,3},{5,4},{6,5},{7,6},{8,7},{9,8},{10,9},{11,1... | collective-permute-start | bytes 1572872 | tf_op jit(solution)/shard_map/ppermute | solution.py:44
  430.0 42.0 %collective-permute-start.25 = (bf16[512,512]{1,0:T(8,128)(2,1)}, bf16[512,512]{1,0:T(8,128)(2,1)}, u32[]{:S(2)}, u32[]{:S(2)}) collective-permute-start(bf16[512,512]{1,0:T(8,128)(2,1)} %bitcast.485), channel_id=1, source_target_pairs={{2,0},{3,1},{4,2},{5,3},{6,4},{7,5},{8,6},{9,7},{10,8},{11,9},{12,... | collective-permute-start | bytes 1572872 | tf_op jit(solution)/shard_map/ppermute | solution.py:44
  449.2 24.0 %collective-permute-start.28 = (bf16[512,512]{1,0:T(8,128)(2,1)}, bf16[512,512]{1,0:T(8,128)(2,1)}, u32[]{:S(2)}, u32[]{:S(2)}) collective-permute-start(bf16[512,512]{1,0:T(8,128)(2,1)} %bitcast.482), channel_id=1, source_target_pairs={{5,0},{6,1},{7,2},{8,3},{9,4},{10,5},{11,6},{12,7},{13,8},{14,9},{... | collective-permute-start | bytes 1572872 | tf_op jit(solution)/shard_map/ppermute | solution.py:44
  450.5 72.7 %collective-permute-start.30 = (bf16[512,512]{1,0:T(8,128)(2,1)}, bf16[512,512]{1,0:T(8,128)(2,1)}, u32[]{:S(2)}, u32[]{:S(2)}) collective-permute-start(bf16[512,512]{1,0:T(8,128)(2,1)} %bitcast.480), channel_id=1, source_target_pairs={{7,0},{8,1},{9,2},{10,3},{11,4},{12,5},{13,6},{14,7},{15,8},{16,9}... | collective-permute-start | bytes 1572872 | tf_op jit(solution)/shard_map/ppermute | solution.py:44
  468.0 62.1 %collective-permute-start.29 = (bf16[512,512]{1,0:T(8,128)(2,1)}, bf16[512,512]{1,0:T(8,128)(2,1)S(1)}, u32[]{:S(2)}, u32[]{:S(2)}) collective-permute-start(bf16[512,512]{1,0:T(8,128)(2,1)} %bitcast.547), channel_id=1, source_target_pairs={{6,0},{7,1},{8,2},{9,3},{10,4},{11,5},{12,6},{13,7},{14,8},{15,9},... | collective-permute-start | bytes 1572872 | tf_op jit(solution)/shard_map/ppermute | solution.py:44
  469.3 63.5 %collective-permute-start.31 = (bf16[512,512]{1,0:T(8,128)(2,1)}, bf16[512,512]{1,0:T(8,128)(2,1)S(1)}, u32[]{:S(2)}, u32[]{:S(2)}) collective-permute-start(bf16[512,512]{1,0:T(8,128)(2,1)} %bitcast.546), channel_id=1, source_target_pairs={{8,0},{9,1},{10,2},{11,3},{12,4},{13,5},{14,6},{15,7},{16,8},{17,9... | collective-permute-start | bytes 1572872 | tf_op jit(solution)/shard_map/ppermute | solution.py:44
  471.9 60.8 %collective-permute-start.26 = (bf16[512,512]{1,0:T(8,128)(2,1)}, bf16[512,512]{1,0:T(8,128)(2,1)S(1)}, u32[]{:S(2)}, u32[]{:S(2)}) collective-permute-start(bf16[512,512]{1,0:T(8,128)(2,1)} %bitcast.545), channel_id=1, source_target_pairs={{3,0},{4,1},{5,2},{6,3},{7,4},{8,5},{9,6},{10,7},{11,8},{12,9},{13... | collective-permute-start | bytes 1572872 | tf_op jit(solution)/shard_map/ppermute | solution.py:44
  473.2 59.5 %collective-permute-start.27 = (bf16[512,512]{1,0:T(8,128)(2,1)}, bf16[512,512]{1,0:T(8,128)(2,1)S(1)}, u32[]{:S(2)}, u32[]{:S(2)}) collective-permute-start(bf16[512,512]{1,0:T(8,128)(2,1)} %bitcast.544), channel_id=1, source_target_pairs={{4,0},{5,1},{6,2},{7,3},{8,4},{9,5},{10,6},{11,7},{12,8},{13,9},{1... | collective-permute-start | bytes 1572872 | tf_op jit(solution)/shard_map/ppermute | solution.py:44
  (49 other events, 688.5 us)
Sparse Core Ops, SparseCore 0:
  540.7 185.9 all-reduce.5
where the time goes:
time: 754 us; the launch traced here: 742 us
  waiting for transfers between devices  300 us (40%)
  local copies, waits for them, and re-layouts  193 us (26%)
  starting transfers between devices  121 us (16%)
  matrix products  65 us (9%)
  other arithmetic  48.3 us (6%)
  between operations  15.3 us (2%)
    psum x1, waiting for transfers between devices, local(): lax.psum(weight_terms[0].astype(jnp.bfloat16), ('dp', 'seq'))  179 us
    ppermute x32, starting transfers between devices, shifted(): return lax.ppermute(block, axis, route)  101 us
    ppermute x32, waiting for transfers between devices, shifted(): return lax.ppermute(block, axis, route)  100 us
    unnamed x142, local copies, waits for them, and re-layouts  76.9 us
    dot_general x19, matrix products, product(): return jnp.einsum(form, left, right, preferred_element_type=jnp.float32)  53.9 us
    all_to_all x1, waiting for transfers between devices, sent_to_all(): lax.all_to_all(jnp.broadcast_to(shard[None], (count, *shard.shape)), axis...  21.3 us
    another operation x9, local copies, waits for them, and re-layouts, bar_block(): jnp.stack(key_parts, 1)  20.7 us
    transpose x2, local copies, waits for them, and re-layouts, product(): return jnp.einsum(form, left, right, preferred_element_type=jnp.float32)  19.7 us
  transfers between devices with their start and end apart: 35, of which 10 were waited for; matrix products, arithmetic and copies ran while one was open for 22% of the time, Pallas kernels for 0%

commit v1 on v0

--- a/solution.py
+++ b/solution.py
@@ -318,7 +318,7 @@
         product("te,td->ed", attended_context, grad_out),
     )
     summed = (
-        lax.psum(weight_terms[0].astype(jnp.bfloat16), ("dp", "seq")).astype(jnp.float32),
+        lax.psum(lax.psum(weight_terms[0].astype(jnp.bfloat16), "seq"), "dp").astype(jnp.float32),
         lax.psum(weight_terms[1].astype(jnp.bfloat16), ("dp", "seq")).astype(jnp.float32),
         lax.psum(weight_terms[2].astype(jnp.bfloat16), ("dp", "seq")).astype(jnp.float32),
         lax.psum(weight_terms[3].astype(jnp.bfloat16), ("dp", "seq")).astype(jnp.float32),

time: 754 us -> 758 us (level)
  waiting for transfers between devices: 300 us -> 283 us
  starting transfers between devices: 121 us -> 133 us
  other arithmetic: 48.3 us -> 56.1 us
    ppermute x32, waiting for transfers between devices: 100 us -> 35.4 us  [shifted(): return lax.ppermute(block, axis, route)]
    psum x1 -> x3, waiting for transfers between devices: 179 us -> 226 us  [the longest x1 166 us: local(): lax.psum(weight_terms[1].astype(jnp.bfloat16), ('dp', 'seq'))]
    all_to_all x1, starting transfers between devices: 14.8 us -> 26.9 us  [sent_and_summed(): lax.all_to_all(parts, axis, split_axis=0, concat_axis=0, tiled=True)]
    unnamed x142 -> x146, local copies, waits for them, and re-layouts: 76.9 us -> 77.6 us
  transfers between devices with their start and end apart: 35 -> 37, of which waited for: 10 -> 11; matrix products, arithmetic and copies ran while one was open for 22% -> 22% of each run, Pallas kernels for 0% -> 0%
where the time goes in v1:
time: 758 us; the launch traced here: 746 us
  waiting for transfers between devices  283 us (37%)
  local copies, waits for them, and re-layouts  195 us (26%)
  starting transfers between devices  133 us (18%)
  matrix products  64.2 us (8%)
  other arithmetic  56.1 us (7%)
  between operations  15.3 us (2%)
    psum x1, waiting for transfers between devices, local(): lax.psum(weight_terms[1].astype(jnp.bfloat16), ('dp', 'seq'))  166 us
    ppermute x32, starting transfers between devices, shifted(): return lax.ppermute(block, axis, route)  102 us
    unnamed x146, local copies, waits for them, and re-layouts  77.6 us
    psum x1, waiting for transfers between devices, local(): lax.psum(weight_terms[0].astype(jnp.bfloat16), 'seq')  57 us
    dot_general x19, matrix products, product(): return jnp.einsum(form, left, right, preferred_element_type=jnp.float32)  52.9 us
    ppermute x32, waiting for transfers between devices, shifted(): return lax.ppermute(block, axis, route)  35.4 us
    all_to_all x1, starting transfers between devices, sent_and_summed(): lax.all_to_all(parts, axis, split_axis=0, concat_axis=0, tiled=True)  26.9 us
    all_to_all x1, waiting for transfers between devices, sent_to_all(): lax.all_to_all(jnp.broadcast_to(shard[None], (count, *shard.shape)), axis...  21.2 us
  transfers between devices with their start and end apart: 37, of which 11 were waited for; matrix products, arithmetic and copies ran while one was open for 22% of the time, Pallas kernels for 0%

profile of v1, /device:TPU:1, one launch (start us, length us, event | category | flops | bytes accessed | tf_op | source)
XLA Modules:
  0.0 746.4 jit_solution(8840447076054307394)
XLA Ops:
  11.3 4.9 collective-permute-start.15
  16.2 4.0 collective-permute-start.14
  20.2 5.3 collective-permute-start.10
  37.0 4.8 all-to-all-start
  56.2 21.2 %all-to-all-done = bf16[32,4,1024]{2,1,0:T(4,128)(2,1)S(1)} async-done(((bf16[32,4,1024]{2,1,0:T(4,128)(2,1)}), bf16[32,4,1024]{2,1,0:T(4,128)(2,1)S(1)}, u32[]{:S(2)}, u32[]{:S(2)}) %all-to-all-start) | async-done | bytes 262176 | tf_op jit(solution)/shard_map/all_to_all | solution.py:16
  85.2 4.2 collective-permute-start.12
  95.4 4.8 collective-permute-start.7
  101.1 11.5 %collective-permute-done.12 = bf16[512,512]{1,0:T(8,128)(2,1)S(1)} collective-permute-done((bf16[512,512]{1,0:T(8,128)(2,1)}, bf16[512,512]{1,0:T(8,128)(2,1)S(1)}, u32[]{:S(2)}, u32[]{:S(2)}) %collective-permute-start.12) | collective-permute-done | bytes 524320 | tf_op jit(solution)/shard_map/ppermute | solution.py:44
  118.3 6.5 collective-permute-start.4
  125.6 5.1 collective-permute-start.1
  136.4 4.7 rev.9
  141.2 7.7 %reshape.379 = bf16[36,128,4,128]{3,2,1,0:T(4,128)(2,1)} reshape(bf16[9,512,512]{2,1,0:T(8,128)(2,1)} %rev.9) | data formatting | bytes 9437184 | tf_op jit(solution)/shard_map/reshape | solution.py:213
  159.1 25.6 %collective-permute-start.3 = (bf16[512,512]{1,0:T(8,128)(2,1)}, bf16[512,512]{1,0:T(8,128)(2,1)}, u32[]{:S(2)}, u32[]{:S(2)}) collective-permute-start(bf16[512,512]{1,0:T(8,128)(2,1)} %get-tuple-element.135), channel_id=1, source_target_pairs={{0,4},{1,5},{2,6},{3,7},{4,8},{5,9},{6,10},{7,11},{8,12},{9,13},{1... | collective-permute-start | bytes 1572872 | tf_op jit(solution)/shard_map/ppermute | solution.py:44
  216.3 5.7 copy.316
  227.6 4.8 rev.8
  232.4 7.7 %reshape.376 = bf16[36,128,4,128]{3,2,1,0:T(4,128)(2,1)} reshape(bf16[9,512,512]{2,1,0:T(8,128)(2,1)} %rev.8) | data formatting | bytes 9437184 | tf_op jit(solution)/shard_map/reshape | solution.py:214
  241.7 4.6 fusion
  275.7 10.1 %fusion.16 = f32[4,128,4,128]{1,3,2,0:T(8,128)} fusion(bf16[4,1152,4,128]{3,1,2,0:T(8,128)(2,1)} %bitcast.13, f32[4,4,128,1152]{3,2,1,0:T(8,128)} %copy-done.1, f32[4,4,128]{2,1,0:T(4,128)S(1)} %copy_add_fusion.1, f32[4,4,128]{2,1,0:T(4,128)S(1)} %copy_maximum_fusion, pred[4,128,1152]{2,1,0:T(8,128)(4,1)S(1)} %broadcast_and_fusion), kind=kOutput, calls=%fused_computation.36 | convolution fusion | flops 618135552 | bytes 15810560 | tf_op jit(solution)/shard_map/while/body/eval_jaxpr/ghqk,gkhe->gqhe/dot_general | solution.py:69
  285.8 8.9 %multiply_reduce_fusion = (f32[4,4,128]{2,1,0:T(4,128)S(1)}, f32[4,4,128,1152]{3,2,1,0:T(8,128)}) fusion(f32[4,4,128]{2,1,0:T(4,128)S(1)} %copy_add_fusion.1, f32[4,4,128]{2,1,0:T(4,128)S(1)} %copy_maximum_fusion, f32[4,4,128,1152]{3,2,1,0:T(8,128)S(1)} %bitcast.496, pred[4,128,1152]{2,1,0:T(8,128)(4,1)S(1)} %broadcast_and_fusion, ...), kind=kOutput, calls=%fused_computation.1 | convolution fusion | flops 620492800 | bytes 24731648 | tf_op jit(solution)/shard_map/while/body/eval_jaxpr/gqhe,gkhe->ghqk/dot_general | solution.py:69
  294.7 5.9 convolution_bitcast_fusion
  302.1 6.6 multiply_convert_fusion
  311.3 4.9 convolution_bitcast_fusion.1
  316.3 9.8 %copy.338 = f32[4,1152,4,128]{3,1,2,0:T(8,128)} copy(f32[4,1152,4,128]{1,3,2,0:T(8,128)} %convolution_bitcast_fusion.1) | data formatting | bytes 18874368 | tf_op jit(solution)/shard_map/while/body/eval_jaxpr/ghqk,gqhe->gkhe/transpose | solution.py:69
  336.7 3.6 fusion.66
  343.5 9.7 %copy.362 = f32[4,1152,4,128]{3,1,2,0:T(8,128)} copy(f32[4,1152,4,128]{1,3,2,0:T(8,128)} %convolution_bitcast_fusion) | data formatting | bytes 18874368 | tf_op jit(solution)/shard_map/while/body/eval_jaxpr/ghqk,gqhe->gkhe/transpose | solution.py:69
  395.4 26.9 %all-to-all-start.1 = ((bf16[32,4,8,128]{3,1,2,0:T(4,128)(2,1)}), bf16[32,4,8,128]{3,1,2,0:T(4,128)(2,1)S(1)}, u32[]{:S(2)}, u32[]{:S(2)}) async-start(bf16[32,4,8,128]{3,1,2,0:T(4,128)(2,1)} %copy.358), calls=%async_computation.1 | async-start | bytes 524288 | tf_op jit(solution)/shard_map/all_to_all | solution.py:55
  429.8 4.8 convert.15
  449.8 3.9 fusion.53
  461.3 57.0 %all-reduce.8.cloned.1.call-done = bf16[1024,512]{0,1:T(8,128)(2,1)} async-done(((bf16[1024,512]{0,1:T(8,128)(2,1)}), bf16[1024,512]{0,1:T(8,128)(2,1)}) %all-reduce.8.cloned.1.call-update) | async-done | bytes 1048592 | tf_op jit(solution)/shard_map/psum | solution.py:321
  529.1 5.9 collective-permute-done.29
  535.0 9.9 %collective-permute-done.31 = bf16[512,512]{1,0:T(8,128)(2,1)} collective-permute-done((bf16[512,512]{1,0:T(8,128)(2,1)}, bf16[512,512]{1,0:T(8,128)(2,1)}, u32[]{:S(2)}, u32[]{:S(2)}) %collective-permute-start.31) | collective-permute-done | bytes 524320 | tf_op jit(solution)/shard_map/ppermute | solution.py:44
  566.8 165.8 %all-reduce.12.cloned.1.call-done = (bf16[1024,512]{0,1:T(8,128)(2,1)}, bf16[1024,512]{0,1:T(8,128)(2,1)}, bf16[512,1024]{1,0:T(8,128)(2,1)}) async-done(((bf16[1024,512]{0,1:T(8,128)(2,1)}, bf16[1024,512]{0,1:T(8,128)(2,1)}, bf16[512,1024]{1,0:T(8,128)(2,1)}), (bf16[1024,512]{0,1:T(8,128)(2,1)}, bf16[1024,512]{0,1:T(8,128)(2,1)}, bf16[512,1024]{1,0:T(8,128)(2,1)})) %all-reduce.12.cloned.1.call-update) | async-done | bytes 3145744 | tf_op jit(solution)/shard_map/psum | solution.py:322
  (340 shorter events, 264.2 us)
Async XLA Ops:
  11.3 121.3 %collective-permute-start.15 = (bf16[512,512]{1,0:T(8,128)(2,1)}, bf16[512,512]{1,0:T(8,128)(2,1)}, u32[]{:S(2)}, u32[]{:S(2)}) collective-permute-start(bf16[512,512]{1,0:T(8,128)(2,1)} %get-tuple-element.137), channel_id=1, source_target_pairs={{0,8},{1,9},{2,10},{3,11},{4,12},{5,13},{6,14},{7,15},{8,16},{9,17... | collective-permute-start | bytes 1572872 | tf_op jit(solution)/shard_map/ppermute | solution.py:44
  16.2 109.4 %collective-permute-start.14 = (bf16[512,512]{1,0:T(8,128)(2,1)}, bf16[512,512]{1,0:T(8,128)(2,1)}, u32[]{:S(2)}, u32[]{:S(2)}) collective-permute-start(bf16[512,512]{1,0:T(8,128)(2,1)} %get-tuple-element.137), channel_id=1, source_target_pairs={{0,7},{1,8},{2,9},{3,10},{4,11},{5,12},{6,13},{7,14},{8,15},{9,16}... | collective-permute-start | bytes 1572872 | tf_op jit(solution)/shard_map/ppermute | solution.py:44
  20.2 71.1 %collective-permute-start.10 = (bf16[512,512]{1,0:T(8,128)(2,1)}, bf16[512,512]{1,0:T(8,128)(2,1)}, u32[]{:S(2)}, u32[]{:S(2)}) collective-permute-start(bf16[512,512]{1,0:T(8,128)(2,1)} %get-tuple-element.137), channel_id=1, source_target_pairs={{0,3},{1,4},{2,5},{3,6},{4,7},{5,8},{6,9},{7,10},{8,11},{9,12},{10... | collective-permute-start | bytes 1572872 | tf_op jit(solution)/shard_map/ppermute | solution.py:44
  25.5 59.7 %collective-permute-start.9 = (bf16[512,512]{1,0:T(8,128)(2,1)}, bf16[512,512]{1,0:T(8,128)(2,1)}, u32[]{:S(2)}, u32[]{:S(2)}) collective-permute-start(bf16[512,512]{1,0:T(8,128)(2,1)} %get-tuple-element.137), channel_id=1, source_target_pairs={{0,2},{1,3},{2,4},{3,5},{4,6},{5,7},{6,8},{7,9},{8,10},{9,11},{10,... | collective-permute-start | bytes 1572872 | tf_op jit(solution)/shard_map/ppermute | solution.py:44
  28.4 52.4 %collective-permute-start.8 = (bf16[512,512]{1,0:T(8,128)(2,1)}, bf16[512,512]{1,0:T(8,128)(2,1)}, u32[]{:S(2)}, u32[]{:S(2)}) collective-permute-start(bf16[512,512]{1,0:T(8,128)(2,1)} %get-tuple-element.137), channel_id=1, source_target_pairs={{0,1},{1,2},{2,3},{3,4},{4,5},{5,6},{6,7},{7,8},{8,9},{9,10},{10,1... | collective-permute-start | bytes 1572872 | tf_op jit(solution)/shard_map/ppermute | solution.py:44
  37.0 40.4 %all-to-all-start = ((bf16[32,4,1024]{2,1,0:T(4,128)(2,1)}), bf16[32,4,1024]{2,1,0:T(4,128)(2,1)S(1)}, u32[]{:S(2)}, u32[]{:S(2)}) async-start(bf16[32,4,1024]{2,1,0:T(4,128)(2,1)} %broadcast_in_dim.191), calls=%async_computation | async-start | bytes 524288 | tf_op jit(solution)/shard_map/all_to_all | solution.py:16
  41.8 476.4 %all-reduce.8.cloned.1.call-start = ((), (), s32[]{:S(2)}) async-start(), calls=%async_computation.2 | async-start | bytes 2097152 | tf_op jit(solution)/shard_map/psum | solution.py:321
  85.2 27.3 %collective-permute-start.12 = (bf16[512,512]{1,0:T(8,128)(2,1)}, bf16[512,512]{1,0:T(8,128)(2,1)S(1)}, u32[]{:S(2)}, u32[]{:S(2)}) collective-permute-start(bf16[512,512]{1,0:T(8,128)(2,1)} %get-tuple-element.137), channel_id=1, source_target_pairs={{0,5},{1,6},{2,7},{3,8},{4,9},{5,10},{6,11},{7,12},{8,13},{9,14},{... | collective-permute-start | bytes 1572872 | tf_op jit(solution)/shard_map/ppermute | solution.py:44
  91.3 26.9 %collective-permute-start.13 = (bf16[512,512]{1,0:T(8,128)(2,1)}, bf16[512,512]{1,0:T(8,128)(2,1)S(1)}, u32[]{:S(2)}, u32[]{:S(2)}) collective-permute-start(bf16[512,512]{1,0:T(8,128)(2,1)} %get-tuple-element.137), channel_id=1, source_target_pairs={{0,6},{1,7},{2,8},{3,9},{4,10},{5,11},{6,12},{7,13},{8,14},{9,15},... | collective-permute-start | bytes 1572872 | tf_op jit(solution)/shard_map/ppermute | solution.py:44
  95.4 130.3 %collective-permute-start.7 = (bf16[512,512]{1,0:T(8,128)(2,1)}, bf16[512,512]{1,0:T(8,128)(2,1)}, u32[]{:S(2)}, u32[]{:S(2)}) collective-permute-start(bf16[512,512]{1,0:T(8,128)(2,1)} %get-tuple-element.135), channel_id=1, source_target_pairs={{0,8},{1,9},{2,10},{3,11},{4,12},{5,13},{6,14},{7,15},{8,16},{9,17... | collective-permute-start | bytes 1572872 | tf_op jit(solution)/shard_map/ppermute | solution.py:44
  112.6 111.3 %collective-permute-start.6 = (bf16[512,512]{1,0:T(8,128)(2,1)}, bf16[512,512]{1,0:T(8,128)(2,1)}, u32[]{:S(2)}, u32[]{:S(2)}) collective-permute-start(bf16[512,512]{1,0:T(8,128)(2,1)} %get-tuple-element.135), channel_id=1, source_target_pairs={{0,7},{1,8},{2,9},{3,10},{4,11},{5,12},{6,13},{7,14},{8,15},{9,16}... | collective-permute-start | bytes 1572872 | tf_op jit(solution)/shard_map/ppermute | solution.py:44
  118.3 78.3 %collective-permute-start.4 = (bf16[512,512]{1,0:T(8,128)(2,1)}, bf16[512,512]{1,0:T(8,128)(2,1)}, u32[]{:S(2)}, u32[]{:S(2)}) collective-permute-start(bf16[512,512]{1,0:T(8,128)(2,1)} %get-tuple-element.135), channel_id=1, source_target_pairs={{0,5},{1,6},{2,7},{3,8},{4,9},{5,10},{6,11},{7,12},{8,13},{9,14},{... | collective-permute-start | bytes 1572872 | tf_op jit(solution)/shard_map/ppermute | solution.py:44
  125.6 33.5 %collective-permute-start.1 = (bf16[512,512]{1,0:T(8,128)(2,1)}, bf16[512,512]{1,0:T(8,128)(2,1)}, u32[]{:S(2)}, u32[]{:S(2)}) collective-permute-start(bf16[512,512]{1,0:T(8,128)(2,1)} %get-tuple-element.135), channel_id=1, source_target_pairs={{0,2},{1,3},{2,4},{3,5},{4,6},{5,7},{6,8},{7,9},{8,10},{9,11},{10,... | collective-permute-start | bytes 1572872 | tf_op jit(solution)/shard_map/ppermute | solution.py:44
  154.9 35.6 %collective-permute-start.2 = (bf16[512,512]{1,0:T(8,128)(2,1)}, bf16[512,512]{1,0:T(8,128)(2,1)}, u32[]{:S(2)}, u32[]{:S(2)}) collective-permute-start(bf16[512,512]{1,0:T(8,128)(2,1)} %get-tuple-element.135), channel_id=1, source_target_pairs={{0,3},{1,4},{2,5},{3,6},{4,7},{5,8},{6,9},{7,10},{8,11},{9,12},{10... | collective-permute-start | bytes 1572872 | tf_op jit(solution)/shard_map/ppermute | solution.py:44
  159.1 35.5 %collective-permute-start.3 = (bf16[512,512]{1,0:T(8,128)(2,1)}, bf16[512,512]{1,0:T(8,128)(2,1)}, u32[]{:S(2)}, u32[]{:S(2)}) collective-permute-start(bf16[512,512]{1,0:T(8,128)(2,1)} %get-tuple-element.135), channel_id=1, source_target_pairs={{0,4},{1,5},{2,6},{3,7},{4,8},{5,9},{6,10},{7,11},{8,12},{9,13},{1... | collective-permute-start | bytes 1572872 | tf_op jit(solution)/shard_map/ppermute | solution.py:44
  190.5 31.5 %collective-permute-start.5 = (bf16[512,512]{1,0:T(8,128)(2,1)}, bf16[512,512]{1,0:T(8,128)(2,1)}, u32[]{:S(2)}, u32[]{:S(2)}) collective-permute-start(bf16[512,512]{1,0:T(8,128)(2,1)} %get-tuple-element.135), channel_id=1, source_target_pairs={{0,6},{1,7},{2,8},{3,9},{4,10},{5,11},{6,12},{7,13},{8,14},{9,15},... | collective-permute-start | bytes 1572872 | tf_op jit(solution)/shard_map/ppermute | solution.py:44
  371.6 68.4 %collective-permute-start.20 = (bf16[512,512]{1,0:T(8,128)(2,1)}, bf16[512,512]{1,0:T(8,128)(2,1)}, u32[]{:S(2)}, u32[]{:S(2)}) collective-permute-start(bf16[512,512]{1,0:T(8,128)(2,1)} %bitcast.490), channel_id=1, source_target_pairs={{5,0},{6,1},{7,2},{8,3},{9,4},{10,5},{11,6},{12,7},{13,8},{14,9},{... | collective-permute-start | bytes 1572872 | tf_op jit(solution)/shard_map/ppermute | solution.py:44
  372.9 68.4 %collective-permute-start.22 = (bf16[512,512]{1,0:T(8,128)(2,1)}, bf16[512,512]{1,0:T(8,128)(2,1)}, u32[]{:S(2)}, u32[]{:S(2)}) collective-permute-start(bf16[512,512]{1,0:T(8,128)(2,1)} %bitcast.488), channel_id=1, source_target_pairs={{7,0},{8,1},{9,2},{10,3},{11,4},{12,5},{13,6},{14,7},{15,8},{16,9}... | collective-permute-start | bytes 1572872 | tf_op jit(solution)/shard_map/ppermute | solution.py:44
  374.2 69.3 %collective-permute-start.21 = (bf16[512,512]{1,0:T(8,128)(2,1)}, bf16[512,512]{1,0:T(8,128)(2,1)}, u32[]{:S(2)}, u32[]{:S(2)}) collective-permute-start(bf16[512,512]{1,0:T(8,128)(2,1)} %bitcast.489), channel_id=1, source_target_pairs={{6,0},{7,1},{8,2},{9,3},{10,4},{11,5},{12,6},{13,7},{14,8},{15,9},... | collective-permute-start | bytes 1572872 | tf_op jit(solution)/shard_map/ppermute | solution.py:44
  375.5 71.5 %collective-permute-start.23 = (bf16[512,512]{1,0:T(8,128)(2,1)}, bf16[512,512]{1,0:T(8,128)(2,1)}, u32[]{:S(2)}, u32[]{:S(2)}) collective-permute-start(bf16[512,512]{1,0:T(8,128)(2,1)} %bitcast.487), channel_id=1, source_target_pairs={{8,0},{9,1},{10,2},{11,3},{12,4},{13,5},{14,6},{15,7},{16,8},{17,9... | collective-permute-start | bytes 1572872 | tf_op jit(solution)/shard_map/ppermute | solution.py:44
  391.0 57.3 %collective-permute-start.18 = (bf16[512,512]{1,0:T(8,128)(2,1)}, bf16[512,512]{1,0:T(8,128)(2,1)}, u32[]{:S(2)}, u32[]{:S(2)}) collective-permute-start(bf16[512,512]{1,0:T(8,128)(2,1)} %bitcast.492), channel_id=1, source_target_pairs={{3,0},{4,1},{5,2},{6,3},{7,4},{8,5},{9,6},{10,7},{11,8},{12,9},{13... | collective-permute-start | bytes 1572872 | tf_op jit(solution)/shard_map/ppermute | solution.py:44
  395.4 130.7 %all-to-all-start.1 = ((bf16[32,4,8,128]{3,1,2,0:T(4,128)(2,1)}), bf16[32,4,8,128]{3,1,2,0:T(4,128)(2,1)S(1)}, u32[]{:S(2)}, u32[]{:S(2)}) async-start(bf16[32,4,8,128]{3,1,2,0:T(4,128)(2,1)} %copy.358), calls=%async_computation.1 | async-start | bytes 524288 | tf_op jit(solution)/shard_map/all_to_all | solution.py:55
  422.4 141.9 %all-reduce.10.cloned.1.call-start = ((), (), s32[]{:S(2)}) async-start(), calls=%async_computation.3 | async-start | bytes 2097152 | tf_op jit(solution)/shard_map/psum | solution.py:321
  440.0 78.3 %collective-permute-start.19 = (bf16[512,512]{1,0:T(8,128)(2,1)}, bf16[512,512]{1,0:T(8,128)(2,1)}, u32[]{:S(2)}, u32[]{:S(2)}) collective-permute-start(bf16[512,512]{1,0:T(8,128)(2,1)} %bitcast.491), channel_id=1, source_target_pairs={{4,0},{5,1},{6,2},{7,3},{8,4},{9,5},{10,6},{11,7},{12,8},{13,9},{1... | collective-permute-start | bytes 1572872 | tf_op jit(solution)/shard_map/ppermute | solution.py:44
  441.3 78.3 %collective-permute-start.16 = (bf16[512,512]{1,0:T(8,128)(2,1)}, bf16[512,512]{1,0:T(8,128)(2,1)}, u32[]{:S(2)}, u32[]{:S(2)}) collective-permute-start(bf16[512,512]{1,0:T(8,128)(2,1)} %bitcast.494), channel_id=1, source_target_pairs={{1,0},{2,1},{3,2},{4,3},{5,4},{6,5},{7,6},{8,7},{9,8},{10,9},{11,1... | collective-permute-start | bytes 1572872 | tf_op jit(solution)/shard_map/ppermute | solution.py:44
  443.5 77.4 %collective-permute-start.25 = (bf16[512,512]{1,0:T(8,128)(2,1)}, bf16[512,512]{1,0:T(8,128)(2,1)}, u32[]{:S(2)}, u32[]{:S(2)}) collective-permute-start(bf16[512,512]{1,0:T(8,128)(2,1)} %bitcast.485), channel_id=1, source_target_pairs={{2,0},{3,1},{4,2},{5,3},{6,4},{7,5},{8,6},{9,7},{10,8},{11,9},{12,... | collective-permute-start | bytes 1572872 | tf_op jit(solution)/shard_map/ppermute | solution.py:44
  447.0 75.2 %collective-permute-start.28 = (bf16[512,512]{1,0:T(8,128)(2,1)}, bf16[512,512]{1,0:T(8,128)(2,1)}, u32[]{:S(2)}, u32[]{:S(2)}) collective-permute-start(bf16[512,512]{1,0:T(8,128)(2,1)} %bitcast.482), channel_id=1, source_target_pairs={{5,0},{6,1},{7,2},{8,3},{9,4},{10,5},{11,6},{12,7},{13,8},{14,9},{... | collective-permute-start | bytes 1572872 | tf_op jit(solution)/shard_map/ppermute | solution.py:44
  448.3 75.2 %collective-permute-start.30 = (bf16[512,512]{1,0:T(8,128)(2,1)}, bf16[512,512]{1,0:T(8,128)(2,1)}, u32[]{:S(2)}, u32[]{:S(2)}) collective-permute-start(bf16[512,512]{1,0:T(8,128)(2,1)} %bitcast.480), channel_id=1, source_target_pairs={{7,0},{8,1},{9,2},{10,3},{11,4},{12,5},{13,6},{14,7},{15,8},{16,9}... | collective-permute-start | bytes 1572872 | tf_op jit(solution)/shard_map/ppermute | solution.py:44
  518.3 214.4 %all-reduce.12.cloned.1.call-start = ((), (), s32[]{:S(2)}) async-start(), calls=%async_computation.4 | async-start | bytes 6291456 | tf_op jit(solution)/shard_map/psum | solution.py:322
  519.6 25.3 %collective-permute-start.31 = (bf16[512,512]{1,0:T(8,128)(2,1)}, bf16[512,512]{1,0:T(8,128)(2,1)}, u32[]{:S(2)}, u32[]{:S(2)}) collective-permute-start(bf16[512,512]{1,0:T(8,128)(2,1)} %bitcast.545), channel_id=1, source_target_pairs={{8,0},{9,1},{10,2},{11,3},{12,4},{13,5},{14,6},{15,7},{16,8},{17,9... | collective-permute-start | bytes 1572872 | tf_op jit(solution)/shard_map/ppermute | solution.py:44
  521.0 26.6 %collective-permute-start.26 = (bf16[512,512]{1,0:T(8,128)(2,1)}, bf16[512,512]{1,0:T(8,128)(2,1)}, u32[]{:S(2)}, u32[]{:S(2)}) collective-permute-start(bf16[512,512]{1,0:T(8,128)(2,1)} %bitcast.544), channel_id=1, source_target_pairs={{3,0},{4,1},{5,2},{6,3},{7,4},{8,5},{9,6},{10,7},{11,8},{12,9},{13... | collective-permute-start | bytes 1572872 | tf_op jit(solution)/shard_map/ppermute | solution.py:44
  522.3 25.8 %collective-permute-start.27 = (bf16[512,512]{1,0:T(8,128)(2,1)}, bf16[512,512]{1,0:T(8,128)(2,1)}, u32[]{:S(2)}, u32[]{:S(2)}) collective-permute-start(bf16[512,512]{1,0:T(8,128)(2,1)} %bitcast.543), channel_id=1, source_target_pairs={{4,0},{5,1},{6,2},{7,3},{8,4},{9,5},{10,6},{11,7},{12,8},{13,9},{1... | collective-permute-start | bytes 1572872 | tf_op jit(solution)/shard_map/ppermute | solution.py:44
  (53 other events, 684.7 us)
Sparse Core Ops, SparseCore 0:
  360.0 158.2 all-reduce.7
  520.7 43.5 all-reduce.9
  570.0 162.6 all-reduce.11
